TPU v7x, 32 devices: a whole 2x2x4 slice. The times are simulated.
32 devices in a mesh: basin: 8 (over z, x), event: 4 (over y, core).
Axes of the slice: x: 2, y: 2, z: 4, core: 2. Of those that a mesh axis runs over, the one named last changes fastest.
Arguments:
- reach_attrs: bfloat16 [12288, 32], P('basin'), may hold values from -6 to 6
- w_first: bfloat16 [32, 768], replicated, may hold values from -1 to 1
- b_first: float32 [768], replicated, may hold values from -3 to 3
- w_second: bfloat16 [768, 768], replicated, may hold values from -0.21875 to 0.21875
- b_second: float32 [768], replicated, may hold values from -3 to 3
- w_out: bfloat16 [768], replicated, may hold values from -0.21875 to 0.21875
- section_factor: float32 [10], replicated, may hold values from 0.5 to 2
- bed_slope: float32 [12288], P('basin'), may hold values from 0.0001 to 0.004
- seg_count: int32 [12288], P('basin'), may hold values from 1 to 8
- section_class: int32 [12288], P('basin'), may hold values from 0 to 9
- down_local: int32 [12288], P('basin'), may hold values from 0 to 1536, as said below
- send_list: int32 [8, 8, 24], P('basin'), may hold values from 0 to 1536, as said below
- recv_list: int32 [8, 8, 24], P('basin'), may hold values from 0 to 1536, as said below
- area_start: float32 [128, 12288], P('event', 'basin'), may hold values from 0.2 to 2
- lateral: float32 [3, 128, 12288], P(None, 'event', 'basin'), may hold values from 0.05 to 1
- cotangent: float32 [128, 12288], P('event', 'basin'), may hold values from -6 to 6
Outputs:
- outflow: float32 [128, 12288], P('event', 'basin')
- grad_lateral: float32 [3, 128, 12288], P(None, 'event', 'basin')
- grad_w_first: float32 [32, 768], replicated
- grad_b_first: float32 [768], replicated
- grad_w_second: float32 [768, 768], replicated
- grad_b_second: float32 [768], replicated
- grad_w_out: float32 [768], replicated
Inputs may be any that keep to these rules, and one draw needn't show every extreme that they name: `down_local`: the downstream reach of a reach in its own sub-basin, as a local index 1 to 8 above the reach's own; 1536 where the reach drains into another sub-basin (it is then listed in send_list) or leaves the network. send_list[s, d, c] is a local reach of sub-basin s whose end flow enters sub-basin d, or 1536 for an empty slot; live slots come first in each list and no reach is listed twice. Only the lists from s to (s + 1), (s + 2), (s + 4) and (s + 7) mod 8 can hold live slots; those to (s + 1), (s + 4) and (s + 7) are always full, the one to (s + 2) is empty or holds 12 or more. One sub-basin receives 24 from each of the four sub-basins that can drain into it. recv_list[d, s, c] is the local reach of sub-basin d that receives slot c of send_list[s, d], and is 1536 exactly where that slot is empty; no reach is a target twice.
All inputs are finite; a program needn't handle non-finite values.
Results may differ from a plain program's by a relative error of at most 0.02.
Values sent between devices are 32-bit elements; how exact they have to be, the bound alone decides.
A program may use at most 64 MiB of HBM per device.

v0:
```python
import math
import jax
import jax.numpy as jnp
from jax import lax
from jax.sharding import PartitionSpec as P

STEPS = 3


def emit(area_now, flow_rate):
    return flow_rate * area_now ** (5.0 / 3.0)


def advance(area_now, inflow, lateral_now, flow_rate, beta_step):
    return (area_now + beta_step * (inflow + lateral_now)) / (
        1.0 + beta_step * flow_rate * area_now ** (2.0 / 3.0)
    )


def network_forward(reach_attrs, w_first, b_first, w_second, b_second, w_out):
    tanh_one = jnp.tanh(jnp.dot(reach_attrs, w_first, preferred_element_type=jnp.float32) + b_first)
    hid_one = tanh_one.astype(jnp.bfloat16)
    tanh_two = jnp.tanh(jnp.dot(hid_one, w_second, preferred_element_type=jnp.float32) + b_second)
    hid_two = tanh_two.astype(jnp.bfloat16)
    squash = jax.nn.sigmoid(jnp.dot(hid_two, w_out, preferred_element_type=jnp.float32))
    return (0.02 + 0.08 * squash, (tanh_one, hid_one, tanh_two, hid_two, squash))


def upper_grads(saved_acts, w_out, g_rough, scale):
    tanh_one, hid_one, tanh_two, hid_two, squash = saved_acts
    g_logit = (g_rough * scale * 0.08 * squash * (1.0 - squash)).astype(jnp.bfloat16)
    grad_w_out = jnp.dot(g_logit, hid_two, preferred_element_type=jnp.float32)
    g_pre_two = (
        g_logit.astype(jnp.float32)[:, None]
        * w_out.astype(jnp.float32)[None, :]
        * (1.0 - tanh_two * tanh_two)
    )
    g_two = g_pre_two.astype(jnp.bfloat16)
    grad_w_second = jnp.dot(hid_one.T, g_two, preferred_element_type=jnp.float32)
    return (g_two, (grad_w_out, jnp.sum(g_pre_two, axis=0), grad_w_second))


def lower_grads(reach_attrs, w_second, saved_acts, g_two):
    tanh_one = saved_acts[0]
    g_pre_one = jnp.dot(g_two, w_second.T, preferred_element_type=jnp.float32) * (
        1.0 - tanh_one * tanh_one
    )
    grad_w_first = jnp.dot(
        reach_attrs.T, g_pre_one.astype(jnp.bfloat16), preferred_element_type=jnp.float32
    )
    return (jnp.sum(g_pre_one, axis=0), grad_w_first)


def body(
    reach_attrs,
    w_first,
    b_first,
    w_second,
    b_second,
    w_out,
    section_factor,
    bed_slope,
    seg_count,
    section_class,
    down_local,
    send_list,
    recv_list,
    area_start,
    lateral,
    cotangent,
):
    local_events, local_reaches = area_start.shape
    class_total = section_factor.shape[0]
    one_hot = (section_class[:, None] == jnp.arange(class_total, dtype=jnp.int32)[None, :]).astype(
        jnp.float32
    )
    k_base = jnp.sqrt(bed_slope) * jnp.sum(one_hot * section_factor[None, :], axis=1)
    beta_step = 1.0 / seg_count.astype(jnp.float32)
    senders = send_list.reshape(-1)
    targets = recv_list.reshape(-1)
    zero_column = jnp.zeros((local_events, 1), jnp.float32)
    roughness, saved_acts = network_forward(
        reach_attrs, w_first, b_first, w_second, b_second, w_out
    )

    def rate_of(rough_all):
        return k_base / rough_all

    flow_rate, pull_rate = jax.vjp(rate_of, roughness)

    def step_of(area_now, inflow, lateral_now, rate_now):
        return advance(area_now, inflow, lateral_now, rate_now, beta_step)

    areas = [area_start]
    inflows = []
    flow_now = emit(area_start, flow_rate)
    for step in range(STEPS):
        confluence_padded = jnp.concatenate([flow_now, zero_column], axis=1)
        confluence_inflow = (
            jnp.zeros((local_events, local_reaches + 1), jnp.float32)
            .at[:, down_local]
            .add(flow_now)
        )
        arrived = lax.all_to_all(
            confluence_padded[:, senders], "basin", split_axis=1, concat_axis=1, tiled=True
        )
        confluence_inflow = confluence_inflow.at[:, targets].add(arrived)
        inflow = confluence_inflow[:, :local_reaches]
        inflows.append(inflow)
        area_next = step_of(areas[step], inflow, lateral[step], flow_rate)
        areas.append(area_next)
        flow_now = emit(area_next, flow_rate)
    g_area, g_rate = jax.vjp(emit, areas[STEPS], flow_rate)[1](cotangent)
    grads_lat = [None] * STEPS
    for step in reversed(range(STEPS)):
        g_prev, g_inflow, g_lateral, g_rate_step = jax.vjp(
            step_of, areas[step], inflows[step], lateral[step], flow_rate
        )[1](g_area)
        grads_lat[step] = g_lateral
        padded = jnp.concatenate([g_inflow, zero_column], axis=1)
        g_flow = jnp.zeros((local_events, local_reaches + 1), jnp.float32)
        returned = lax.all_to_all(
            padded[:, targets], "basin", split_axis=1, concat_axis=1, tiled=True
        )
        g_flow = g_flow.at[:, senders].add(returned)
        g_flow = g_flow[:, :local_reaches] + padded[:, down_local]
        g_emit_area, g_emit_rate = jax.vjp(emit, areas[step], flow_rate)[1](g_flow)
        g_area = g_prev + g_emit_area
        g_rate = g_rate + g_rate_step + g_emit_rate
    grad_lateral = jnp.stack(grads_lat, axis=0)
    g_rough = pull_rate(g_rate)[0]
    scale = 32.0 / math.sqrt(
        local_events * lax.axis_size("event") * local_reaches * lax.axis_size("basin")
    )
    g_two, upper = upper_grads(saved_acts, w_out, g_rough, scale)
    upper = lax.psum((upper[0], upper[1], upper[2]), ("basin", "event"))
    lower = lax.psum(lower_grads(reach_attrs, w_second, saved_acts, g_two), ("basin", "event"))
    grad_w_out, grad_b_second, grad_w_second = upper
    grad_b_first, grad_w_first = lower
    return (
        flow_now,
        grad_lateral,
        grad_w_first,
        grad_b_first,
        grad_w_second,
        grad_b_second,
        grad_w_out,
    )


def solution(mesh):
    return jax.shard_map(
        body,
        mesh=mesh,
        in_specs=(
            P("basin", None),
            P(),
            P(),
            P(),
            P(),
            P(),
            P(),
            P("basin"),
            P("basin"),
            P("basin"),
            P("basin"),
            P("basin", None, None),
            P("basin", None, None),
            P("event", "basin"),
            P(None, "event", "basin"),
            P("event", "basin"),
        ),
        out_specs=(P("event", "basin"), P(None, "event", "basin"), P(), P(), P(), P(), P()),
        check_vma=False,
    )
```

profile of v0, /device:TPU:0, one launch (start us, length us, event | category | flops | bytes accessed | tf_op | source)
XLA Modules:
  0.0 334.1 jit_solution(14651421957676418809)
XLA Ops:
  9.9 2.1 fusion.13
  12.0 2.1 copy-done.1
  18.8 7.3 %all-to-all-start = ((f32[8,1,768]{2,1,0:T(1,128)}), f32[8,1,768]{2,1,0:T(1,128)}, u32[]{:S(2)}, u32[]{:S(2)}) async-start(f32[8,1,768]{2,1,0:T(1,128)} %reshape.288), calls=%async_computation | async-start | bytes 49152 | tf_op jit(solution)/shard_map/all_to_all | solution.py:104
  29.0 9.0 %scatter_custom_fusion = f32[32,1537]{0,1:T(8,128)S(1)} fusion(s32[1536]{0:T(1024)} %compare_select_fusion, f32[1536,32]{1,0:T(8,128)S(1)} %copy.57, f32[]{:T(128)} %constant.11.clone.1), kind=kCustom, calls=%fused_computation.44 | custom fusion | flops 49152 | bytes 197248 | tf_op jit(solution)/shard_map/scatter-add | solution.py:102
  40.1 2.0 scatter_fusion
  45.5 2.0 gather_fusion.1
  48.2 6.1 %all-to-all-start.1 = ((f32[8,1,768]{2,1,0:T(1,128)}), f32[8,1,768]{2,1,0:T(1,128)S(1)}, u32[]{:S(2)}, u32[]{:S(2)}) async-start(f32[8,1,768]{2,1,0:T(1,128)} %reshape.290), calls=%async_computation.1 | async-start | bytes 49152 | tf_op jit(solution)/shard_map/all_to_all | solution.py:104
  55.4 9.3 %scatter_custom_fusion.2 = f32[32,1537]{0,1:T(8,128)S(1)} fusion(s32[1536]{0:T(1024)} %compare_select_fusion, f32[1536,32]{1,0:T(8,128)} %copy.60, f32[]{:T(128)} %constant.11.clone.1), kind=kCustom, calls=%fused_computation.42 | custom fusion | flops 49152 | bytes 197248 | tf_op jit(solution)/shard_map/scatter-add | solution.py:102
  65.5 2.1 scatter_fusion.1
  73.3 6.1 %all-to-all-start.2 = ((f32[8,1,768]{2,1,0:T(1,128)}), f32[8,1,768]{2,1,0:T(1,128)S(1)}, u32[]{:S(2)}, u32[]{:S(2)}) async-start(f32[8,1,768]{2,1,0:T(1,128)} %reshape.292), calls=%async_computation.2 | async-start | bytes 49152 | tf_op jit(solution)/shard_map/all_to_all | solution.py:104
  81.8 9.3 %scatter_custom_fusion.4 = f32[32,1537]{0,1:T(8,128)S(1)} fusion(s32[1536]{0:T(1024)} %compare_select_fusion, f32[1536,32]{1,0:T(8,128)} %copy.63, f32[]{:T(128)} %constant.11.clone.1), kind=kCustom, calls=%fused_computation.40 | custom fusion | flops 49152 | bytes 197248 | tf_op jit(solution)/shard_map/scatter-add | solution.py:102
  91.9 2.0 scatter_fusion.2
  103.3 6.1 %all-to-all-start.3 = ((f32[8,1,768]{2,1,0:T(1,128)}), f32[8,1,768]{2,1,0:T(1,128)}, u32[]{:S(2)}, u32[]{:S(2)}) async-start(f32[8,1,768]{2,1,0:T(1,128)} %reshape.294), calls=%async_computation.3 | async-start | bytes 49152 | tf_op jit(solution)/shard_map/all_to_all | solution.py:122
  110.7 4.0 %gather_fusion.4 = f32[1536,32]{1,0:T(8,128)} fusion(f32[32,1537]{0,1:T(8,128)S(1)} %concatenate.21.clone, s32[2048]{0:T(1024)} %pad_clamp_fusion), kind=kCustom, calls=%fused_computation.4 | custom fusion | bytes 399360 | tf_op jit(solution)/shard_map/gather | solution.py:126
  114.7 2.0 copy.69
  118.9 2.1 scatter_custom_fusion.6
  123.3 3.3 fusion.41
  132.6 5.9 %all-to-all-start.4 = ((f32[8,1,768]{2,1,0:T(1,128)}), f32[8,1,768]{2,1,0:T(1,128)}, u32[]{:S(2)}, u32[]{:S(2)}) async-start(f32[8,1,768]{2,1,0:T(1,128)} %reshape.296), calls=%async_computation.4 | async-start | bytes 49152 | tf_op jit(solution)/shard_map/all_to_all | solution.py:122
  138.6 4.0 %gather_fusion.6 = f32[1536,32]{1,0:T(8,128)} fusion(f32[32,1537]{0,1:T(8,128)S(1)} %concatenate.22.clone, s32[2048]{0:T(1024)} %pad_clamp_fusion), kind=kCustom, calls=%fused_computation.6 | custom fusion | bytes 399360 | tf_op jit(solution)/shard_map/gather | solution.py:126
  142.6 2.1 copy.73
  147.5 2.3 scatter_custom_fusion.7
  152.1 3.2 multiply_reduce_fusion.4
  158.3 5.3 %all-to-all-start.5 = ((f32[8,1,768]{2,1,0:T(1,128)}), f32[8,1,768]{2,1,0:T(1,128)S(1)}, u32[]{:S(2)}, u32[]{:S(2)}) async-start(f32[8,1,768]{2,1,0:T(1,128)} %reshape.298), calls=%async_computation.5 | async-start | bytes 49152 | tf_op jit(solution)/shard_map/all_to_all | solution.py:122
  164.3 3.0 gather_fusion.8
  167.6 2.7 all-to-all-done.5
  173.5 7.0 %fusion.51 = (f32[768]{0:T(1024)S(1)}, bf16[1536,768]{1,0:T(8,128)(2,1)S(1)}) fusion(f32[1536,768]{1,0:T(8,128)} %copy-done.3, f32[768]{0:T(1024)S(1)} %copy-done.37, bf16[768,768]{1,0:T(8,128)(2,1)S(1)} %copy-done, f32[1536,768]{1,0:T(8,128)} %copy-done.1, f32[768]{0:T(1024)S(1)} %convert_element_type.30, f32[1536]{0:T(1024)S(1)} %get-tuple-element.38, ...), kind=kOutput, calls=%fused_computation.102 | convolution fusion | flops 1826094336 | bytes 12994560 | tf_op jit(solution)/shard_map/dot_general | solution.py:45
  180.6 6.2 %fusion.11 = f32[768,768]{1,0:T(8,128)} fusion(f32[1536,768]{1,0:T(8,128)} %copy-done.3, f32[768]{0:T(1024)S(1)} %copy-done.37, f32[1536,768]{1,0:T(8,128)S(1)} %bitcast.127, f32[768]{0:T(1024)S(1)} %convert_element_type.30, f32[1536]{0:T(1024)S(1)} %get-tuple-element.38, f32[768]{0:T(1024)S(1)} %copy-done.20), kind=kOutput, calls=%fused_computation.31 | convolution fusion | flops 1821376512 | bytes 11811840 | tf_op jit(solution)/shard_map/dot_general | solution.py:39
  188.8 3.1 convolution_reduce_fusion.1
  191.9 3.6 %fusion.2 = f32[768]{0:T(1024)S(1)} fusion(f32[1536,768]{1,0:T(8,128)} %copy-done.1, f32[768]{0:T(1024)S(1)} %convert_element_type.30, f32[1536]{0:T(1024)S(1)} %get-tuple-element.38, f32[768]{0:T(1024)S(1)} %copy-done.20), kind=kLoop, calls=%fused_computation.24 | loop fusion | flops 7077120 | bytes 4733952 | tf_op jit(solution)/shard_map/reduce_sum | solution.py:40
  195.4 38.7 %all-reduce.6 = (f32[768]{0:T(1024)}, f32[768]{0:T(1024)}, f32[768]{0:T(1024)}) all-reduce(f32[768]{0:T(1024)S(1)} %get-tuple-element.54, f32[768]{0:T(1024)S(1)} %fusion.2, f32[768]{0:T(1024)S(1)} %convolution_reduce_fusion.1), channel_id=1, replica_groups=mesh['basin'=8,'event'=4] {'basin','event'}, use_global_device_ids=true, to_apply=%region_19.0 | all-reduce | flops 2304 | bytes 18432 | tf_op jit(solution)/shard_map/psum | solution.py:137
  234.2 88.4 %all-reduce.10.cloned.1.call-done = (f32[32,768]{1,0:T(8,128)}, f32[768,768]{1,0:T(8,128)}) async-done(((f32[32,768]{1,0:T(8,128)}, f32[768,768]{1,0:T(8,128)}), (f32[32,768]{1,0:T(8,128)}, f32[768,768]{1,0:T(8,128)})) %all-reduce.10.cloned.1.call-update) | async-done | bytes 2457616 | tf_op jit(solution)/shard_map/psum | solution.py:137
  324.1 3.2 copy.96
  (166 shorter events, 63.8 us)
Async XLA Ops:
  7.2 2.7 copy-start
  7.2 2.5 copy-start.35
  7.2 2.6 copy-start.36
  9.8 5.0 %copy-start.18 = (f32[1536]{0:T(1024)}, f32[1536]{0:T(1024)S(1)}, u32[]{:S(2)}) copy-start(f32[1536]{0:T(1024)S(1)} %select_reduce_fusion) | copy-start | bytes 18436
  9.9 4.2 %copy-start.20 = (f32[768]{0:T(1024)S(1)}, f32[768]{0:T(1024)}, u32[]{:S(2)}) copy-start(f32[768]{0:T(1024)} %param.20) | copy-start | bytes 9220
  14.9 27.6 %copy-start.4 = (f32[3,32,1536]{2,1,0:T(8,128)S(1)}, f32[3,32,1536]{2,1,0:T(8,128)}, u32[]{:S(2)}) copy-start(f32[3,32,1536]{2,1,0:T(8,128)} %param.30) | copy-start | bytes 1769476
  18.8 19.3 %all-to-all-start = ((f32[8,1,768]{2,1,0:T(1,128)}), f32[8,1,768]{2,1,0:T(1,128)}, u32[]{:S(2)}, u32[]{:S(2)}) async-start(f32[8,1,768]{2,1,0:T(1,128)} %reshape.288), calls=%async_computation | async-start | bytes 49152 | tf_op jit(solution)/shard_map/all_to_all | solution.py:104
  42.5 23.0 %copy-start.31 = (s32[192,1]{0,1:T(1,128)S(1)}, s32[192,1]{0,1:T(1,128)}, u32[]{:S(2)}) copy-start(s32[192,1]{0,1:T(1,128)} %compare_select_fusion.2) | copy-start | bytes 2308
  48.2 16.5 %all-to-all-start.1 = ((f32[8,1,768]{2,1,0:T(1,128)}), f32[8,1,768]{2,1,0:T(1,128)S(1)}, u32[]{:S(2)}, u32[]{:S(2)}) async-start(f32[8,1,768]{2,1,0:T(1,128)} %reshape.290), calls=%async_computation.1 | async-start | bytes 49152 | tf_op jit(solution)/shard_map/all_to_all | solution.py:104
  67.9 28.3 %copy-start.6 = (f32[32,1536]{1,0:T(8,128)S(1)}, f32[32,1536]{1,0:T(8,128)}, u32[]{:S(2)}) copy-start(f32[32,1536]{1,0:T(8,128)} %param.31) | copy-start | bytes 589828
  67.9 28.3 %copy-start.13 = (f32[1536]{0:T(1024)S(1)}, f32[1536]{0:T(1024)}, u32[]{:S(2)}) copy-start(f32[1536]{0:T(1024)} %get-tuple-element.49) | copy-start | bytes 18436
  67.9 28.3 %copy-start.14 = (f32[1536]{0:T(1024)S(1)}, f32[1536]{0:T(1024)}, u32[]{:S(2)}) copy-start(f32[1536]{0:T(1024)} %get-tuple-element.53) | copy-start | bytes 18436
  73.3 17.8 %all-to-all-start.2 = ((f32[8,1,768]{2,1,0:T(1,128)}), f32[8,1,768]{2,1,0:T(1,128)S(1)}, u32[]{:S(2)}, u32[]{:S(2)}) async-start(f32[8,1,768]{2,1,0:T(1,128)} %reshape.292), calls=%async_computation.2 | async-start | bytes 49152 | tf_op jit(solution)/shard_map/all_to_all | solution.py:104
  97.3 26.1 %copy-start.5 = (f32[32,1536]{1,0:T(8,128)S(1)}, f32[32,1536]{1,0:T(8,128)}, u32[]{:S(2)}) copy-start(f32[32,1536]{1,0:T(8,128)} %get-tuple-element.48) | copy-start | bytes 589828
  103.3 13.4 %all-to-all-start.3 = ((f32[8,1,768]{2,1,0:T(1,128)}), f32[8,1,768]{2,1,0:T(1,128)}, u32[]{:S(2)}, u32[]{:S(2)}) async-start(f32[8,1,768]{2,1,0:T(1,128)} %reshape.294), calls=%async_computation.3 | async-start | bytes 49152 | tf_op jit(solution)/shard_map/all_to_all | solution.py:122
  132.6 12.7 %all-to-all-start.4 = ((f32[8,1,768]{2,1,0:T(1,128)}), f32[8,1,768]{2,1,0:T(1,128)}, u32[]{:S(2)}, u32[]{:S(2)}) async-start(f32[8,1,768]{2,1,0:T(1,128)} %reshape.296), calls=%async_computation.4 | async-start | bytes 49152 | tf_op jit(solution)/shard_map/all_to_all | solution.py:122
  156.6 16.8 %copy-start.17 = (f32[1536]{0:T(1024)S(1)}, f32[1536]{0:T(1024)}, u32[]{:S(2)}) copy-start(f32[1536]{0:T(1024)} %copy-done.16) | copy-start | bytes 18436
  156.6 16.8 %copy-start.19 = (f32[1536]{0:T(1024)S(1)}, f32[1536]{0:T(1024)}, u32[]{:S(2)}) copy-start(f32[1536]{0:T(1024)} %copy-done.18) | copy-start | bytes 18436
  156.6 16.8 %copy-start.21 = (f32[1536]{0:T(1024)S(1)}, f32[1536]{0:T(1024)}, u32[]{:S(2)}) copy-start(f32[1536]{0:T(1024)} %get-tuple-element.51) | copy-start | bytes 18436
  156.6 16.8 %copy-start.22 = (f32[1536]{0:T(1024)S(1)}, f32[1536]{0:T(1024)}, u32[]{:S(2)}) copy-start(f32[1536]{0:T(1024)} %get-tuple-element.28) | copy-start | bytes 18436
  156.6 16.8 %copy-start.23 = (f32[1536]{0:T(1024)S(1)}, f32[1536]{0:T(1024)}, u32[]{:S(2)}) copy-start(f32[1536]{0:T(1024)} %get-tuple-element.29) | copy-start | bytes 18436
  156.6 16.8 %copy-start.24 = (f32[1536]{0:T(1024)S(1)}, f32[1536]{0:T(1024)}, u32[]{:S(2)}) copy-start(f32[1536]{0:T(1024)} %get-tuple-element.30) | copy-start | bytes 18436
  156.6 16.8 %copy-start.25 = (f32[1536]{0:T(1024)S(1)}, f32[1536]{0:T(1024)}, u32[]{:S(2)}) copy-start(f32[1536]{0:T(1024)} %get-tuple-element.31) | copy-start | bytes 18436
  156.6 16.8 %copy-start.26 = (f32[1536]{0:T(1024)S(1)}, f32[1536]{0:T(1024)}, u32[]{:S(2)}) copy-start(f32[1536]{0:T(1024)} %get-tuple-element.32) | copy-start | bytes 18436
  156.6 16.8 %copy-start.28 = (s32[1536]{0:T(1024)S(1)}, s32[1536]{0:T(1024)}, u32[]{:S(2)}) copy-start(s32[1536]{0:T(1024)} %param.24) | copy-start | bytes 18436
  156.7 16.8 %copy-start.30 = (f32[1536]{0:T(1024)S(1)}, f32[1536]{0:T(1024)}, u32[]{:S(2)}) copy-start(f32[1536]{0:T(1024)} %param.23) | copy-start | bytes 18436
  156.7 16.9 %copy-start.37 = (f32[768]{0:T(1024)S(1)}, f32[768]{0:T(1024)}, u32[]{:S(2)}) copy-start(f32[768]{0:T(1024)} %param.18) | copy-start | bytes 9220
  158.3 11.9 %all-to-all-start.5 = ((f32[8,1,768]{2,1,0:T(1,128)}), f32[8,1,768]{2,1,0:T(1,128)S(1)}, u32[]{:S(2)}, u32[]{:S(2)}) async-start(f32[8,1,768]{2,1,0:T(1,128)} %reshape.298), calls=%async_computation.5 | async-start | bytes 49152 | tf_op jit(solution)/shard_map/all_to_all | solution.py:122
  163.6 158.9 %all-reduce.10.cloned.1.call-start = ((), (), s32[]{:S(2)}) async-start(), calls=%async_computation.6 | async-start | bytes 4915200 | tf_op jit(solution)/shard_map/psum | solution.py:137
  173.0 7.5 %slice-start = ((s8[4718592]{0:T(1024)(128)(4,1)}), s8[524288]{0:T(1024)(128)(4,1)S(1)}, s32[]{:S(2)}) async-start(s8[4718592]{0:T(1024)(128)(4,1)} %bitcast.126), calls=%async_computation.7 | async-start | bytes 1048576
  173.5 7.0 %slice-start.1 = ((s8[4718592]{0:T(1024)(128)(4,1)}), s8[4194304]{0:T(1024)(128)(4,1)S(1)}, s32[]{:S(2)}) async-start(s8[4718592]{0:T(1024)(128)(4,1)} %bitcast.126), calls=%async_computation.8 | async-start | bytes 8388608
  180.5 6.2 %copy-start.15 = (bf16[1536,32]{0,1:T(8,128)(2,1)S(1)}, bf16[1536,32]{0,1:T(8,128)(2,1)}, u32[]{:S(2)}) copy-start(bf16[1536,32]{0,1:T(8,128)(2,1)} %param.16) | copy-start | bytes 294916
  (15 other events, 19.9 us)
Sparse Core Ops, SparseCore 0:
  188.0 134.4 all-reduce.9
where the time goes:
time: 336 us; the launch traced here: 334 us
  waiting for transfers between devices  91.7 us (27%)
  other arithmetic  69.4 us (21%)
  local copies, waits for them, and re-layouts  60.8 us (18%)
  blocking collectives  38.7 us (12%)
  starting transfers between devices  36.8 us (11%)
  matrix products  21.9 us (7%)
  between operations  14.9 us (4%)
    psum x1, waiting for transfers between devices, body(): lax.psum(lower_grads(reach_attrs, w_second, saved_acts, g_two), ('basin',...  88.4 us
    psum x1, blocking collectives, body(): lax.psum(lower_grads(reach_attrs, w_second, saved_acts, g_two), ('basin',...  38.7 us
    scatter-add x3, other arithmetic, body(): confluence_inflow = jnp.zeros((local_events, local_reaches + 1), jnp.floa...  27.6 us
    unnamed x107, local copies, waits for them, and re-layouts  25.7 us
    all_to_all x3, starting transfers between devices, body(): lax.all_to_all(confluence_padded[:, senders], 'basin', split_axis=1, conc...  19.4 us
    all_to_all x3, starting transfers between devices, body(): lax.all_to_all(padded[:, targets], 'basin', split_axis=1, concat_axis=1,...  17.3 us
    gather x6, local copies, waits for them, and re-layouts, body(): g_flow = g_flow[:, :local_reaches] + padded[:, down_local]  15.3 us
    dot_general x1, matrix products, lower_grads(): jnp.dot(g_two, w_second.T, preferred_element_type=jnp.float32)  6.97 us
  transfers between devices with their start and end apart: 7, of which 3 were waited for; matrix products, arithmetic and copies ran while one was open for 18% of the time, Pallas kernels for 0%

commit v1 on v0

--- a/solution.py
+++ b/solution.py
@@ -134,7 +134,8 @@
     )
     g_two, upper = upper_grads(saved_acts, w_out, g_rough, scale)
     upper = lax.psum((upper[0], upper[1], upper[2]), ("basin", "event"))
-    lower = lax.psum(lower_grads(reach_attrs, w_second, saved_acts, g_two), ("basin", "event"))
+    local_block = lower_grads(reach_attrs, w_second, saved_acts, g_two)
+    lower = lax.psum(lax.psum(local_block, "event"), "basin")
     grad_w_out, grad_b_second, grad_w_second = upper
     grad_b_first, grad_w_first = lower
     return (

time: 336 us -> 441 us (1.31)
  waiting for transfers between devices: 91.7 us -> 166 us
  blocking collectives: 38.7 us -> 66.9 us
    psum x1 -> x3, waiting for transfers between devices: 88.4 us -> 163 us  [the longest x1 132 us: body(): upper = lax.psum((upper[0], upper[1], upper[2]), ('basin', 'event'))]
    psum x1 -> x3, blocking collectives: 38.7 us -> 66.9 us  [the longest x1 39.5 us: body(): upper = lax.psum((upper[0], upper[1], upper[2]), ('basin', 'event'))]
    unnamed x107 -> x87, local copies, waits for them, and re-layouts: 25.7 us -> 25.7 us
  transfers between devices with their start and end apart: 7 -> 9, of which waited for: 3 -> 4; matrix products, arithmetic and copies ran while one was open for 18% -> 15% of each run, Pallas kernels for 0% -> 0%
where the time goes in v1:
time: 441 us; the launch traced here: 439 us
  waiting for transfers between devices  166 us (38%)
  other arithmetic  70.5 us (16%)
  blocking collectives  66.9 us (15%)
  local copies, waits for them, and re-layouts  60.7 us (14%)
  starting transfers between devices  37.1 us (8%)
  matrix products  23.3 us (5%)
  between operations  14.4 us (3%)
    psum x1, waiting for transfers between devices, body(): upper = lax.psum((upper[0], upper[1], upper[2]), ('basin', 'event'))  132 us
    psum x1, blocking collectives, body(): upper = lax.psum((upper[0], upper[1], upper[2]), ('basin', 'event'))  39.5 us
    psum x2, waiting for transfers between devices, body(): lower = lax.psum(lax.psum(local_block, 'event'), 'basin')  30.7 us
    scatter-add x3, other arithmetic, body(): confluence_inflow = jnp.zeros((local_events, local_reaches + 1), jnp.floa...  27.6 us
    psum x2, blocking collectives, body(): lower = lax.psum(lax.psum(local_block, 'event'), 'basin')  27.3 us
    unnamed x87, local copies, waits for them, and re-layouts  25.7 us
    all_to_all x3, starting transfers between devices, body(): lax.all_to_all(confluence_padded[:, senders], 'basin', split_axis=1, conc...  19.4 us
    all_to_all x3, starting transfers between devices, body(): lax.all_to_all(padded[:, targets], 'basin', split_axis=1, concat_axis=1,...  17.6 us
  transfers between devices with their start and end apart: 9, of which 4 were waited for; matrix products, arithmetic and copies ran while one was open for 15% of the time, Pallas kernels for 0%

profile of v1, /device:TPU:0, one launch (start us, length us, event | category | flops | bytes accessed | tf_op | source)
XLA Modules:
  0.0 438.6 jit_solution(7729788527165779916)
XLA Ops:
  9.9 2.1 fusion.13
  12.0 2.1 copy-done.1
  18.8 7.3 %all-to-all-start = ((f32[8,1,768]{2,1,0:T(1,128)}), f32[8,1,768]{2,1,0:T(1,128)}, u32[]{:S(2)}, u32[]{:S(2)}) async-start(f32[8,1,768]{2,1,0:T(1,128)} %reshape.288), calls=%async_computation | async-start | bytes 49152 | tf_op jit(solution)/shard_map/all_to_all | solution.py:104
  29.0 9.0 %scatter_custom_fusion = f32[32,1537]{0,1:T(8,128)S(1)} fusion(s32[1536]{0:T(1024)} %compare_select_fusion, f32[1536,32]{1,0:T(8,128)S(1)} %copy.57, f32[]{:T(128)} %constant.11.clone.1), kind=kCustom, calls=%fused_computation.44 | custom fusion | flops 49152 | bytes 197248 | tf_op jit(solution)/shard_map/scatter-add | solution.py:102
  48.2 6.1 %all-to-all-start.1 = ((f32[8,1,768]{2,1,0:T(1,128)}), f32[8,1,768]{2,1,0:T(1,128)S(1)}, u32[]{:S(2)}, u32[]{:S(2)}) async-start(f32[8,1,768]{2,1,0:T(1,128)} %reshape.290), calls=%async_computation.1 | async-start | bytes 49152 | tf_op jit(solution)/shard_map/all_to_all | solution.py:104
  55.4 9.3 %scatter_custom_fusion.2 = f32[32,1537]{0,1:T(8,128)S(1)} fusion(s32[1536]{0:T(1024)} %compare_select_fusion, f32[1536,32]{1,0:T(8,128)} %copy.60, f32[]{:T(128)} %constant.11.clone.1), kind=kCustom, calls=%fused_computation.42 | custom fusion | flops 49152 | bytes 197248 | tf_op jit(solution)/shard_map/scatter-add | solution.py:102
  65.5 2.1 scatter_fusion.1
  73.3 6.1 %all-to-all-start.2 = ((f32[8,1,768]{2,1,0:T(1,128)}), f32[8,1,768]{2,1,0:T(1,128)S(1)}, u32[]{:S(2)}, u32[]{:S(2)}) async-start(f32[8,1,768]{2,1,0:T(1,128)} %reshape.292), calls=%async_computation.2 | async-start | bytes 49152 | tf_op jit(solution)/shard_map/all_to_all | solution.py:104
  81.8 9.3 %scatter_custom_fusion.4 = f32[32,1537]{0,1:T(8,128)S(1)} fusion(s32[1536]{0:T(1024)} %compare_select_fusion, f32[1536,32]{1,0:T(8,128)} %copy.63, f32[]{:T(128)} %constant.11.clone.1), kind=kCustom, calls=%fused_computation.40 | custom fusion | flops 49152 | bytes 197248 | tf_op jit(solution)/shard_map/scatter-add | solution.py:102
  103.3 6.1 %all-to-all-start.3 = ((f32[8,1,768]{2,1,0:T(1,128)}), f32[8,1,768]{2,1,0:T(1,128)}, u32[]{:S(2)}, u32[]{:S(2)}) async-start(f32[8,1,768]{2,1,0:T(1,128)} %reshape.294), calls=%async_computation.3 | async-start | bytes 49152 | tf_op jit(solution)/shard_map/all_to_all | solution.py:122
  110.7 4.0 gather_fusion.4
  114.7 2.0 copy.69
  118.9 2.1 scatter_custom_fusion.6
  123.3 3.3 fusion.41
  132.7 5.9 %all-to-all-start.4 = ((f32[8,1,768]{2,1,0:T(1,128)}), f32[8,1,768]{2,1,0:T(1,128)}, u32[]{:S(2)}, u32[]{:S(2)}) async-start(f32[8,1,768]{2,1,0:T(1,128)} %reshape.296), calls=%async_computation.4 | async-start | bytes 49152 | tf_op jit(solution)/shard_map/all_to_all | solution.py:122
  138.6 4.0 gather_fusion.6
  142.6 2.1 copy.73
  147.5 2.1 scatter_custom_fusion.7
  151.9 3.2 multiply_reduce_fusion.4
  158.0 5.5 %all-to-all-start.5 = ((f32[8,1,768]{2,1,0:T(1,128)}), f32[8,1,768]{2,1,0:T(1,128)S(1)}, u32[]{:S(2)}, u32[]{:S(2)}) async-start(f32[8,1,768]{2,1,0:T(1,128)} %reshape.298), calls=%async_computation.5 | async-start | bytes 49152 | tf_op jit(solution)/shard_map/all_to_all | solution.py:122
  164.8 3.0 gather_fusion.8
  168.1 2.1 all-to-all-done.5
  174.2 6.9 %fusion.51 = (f32[768]{0:T(1024)S(1)}, bf16[1536,768]{1,0:T(8,128)(2,1)S(1)}) fusion(f32[1536,768]{1,0:T(8,128)} %copy-done.3, f32[768]{0:T(1024)} %param.18, bf16[768,768]{1,0:T(8,128)(2,1)S(1)} %copy-done, f32[1536,768]{1,0:T(8,128)} %copy-done.1, f32[768]{0:T(1024)} %convert_element_type.30, f32[1536]{0:T(1024)S(1)} %get-tuple-element.35, ...), kind=kOutput, calls=%fused_computation.102 | convolution fusion | flops 1826094336 | bytes 12994560 | tf_op jit(solution)/shard_map/dot_general | solution.py:45
  182.3 30.7 %all-reduce.11.cloned.1.call-done = f32[32,768]{1,0:T(8,128)} async-done(((f32[32,768]{1,0:T(8,128)}), f32[32,768]{1,0:T(8,128)}) %all-reduce.11.cloned.1.call-update) | async-done | bytes 98320 | tf_op jit(solution)/shard_map/psum | solution.py:138
  213.1 7.7 %fusion.11 = f32[768,768]{1,0:T(8,128)} fusion(f32[1536,768]{1,0:T(8,128)} %copy-done.3, f32[768]{0:T(1024)S(1)} %copy-done.29, f32[1536,768]{1,0:T(8,128)} %copy-done.1, f32[768]{0:T(1024)S(1)} %copy-done.23, f32[1536]{0:T(1024)S(1)} %get-tuple-element.35, f32[768]{0:T(1024)S(1)} %copy-done.19), kind=kOutput, calls=%fused_computation.31 | convolution fusion | flops 1821376512 | bytes 11811840 | tf_op jit(solution)/shard_map/dot_general | solution.py:39
  221.6 3.1 convolution_reduce_fusion.1
  224.7 3.5 fusion.2
  228.2 39.5 %all-reduce.6 = (f32[768]{0:T(1024)}, f32[768]{0:T(1024)}) all-reduce(f32[768]{0:T(1024)S(1)} %fusion.2, f32[768]{0:T(1024)S(1)} %convolution_reduce_fusion.1), channel_id=1, replica_groups=mesh['basin'=8,'event'=4] {'basin','event'}, use_global_device_ids=true, to_apply=%region_24.0 | all-reduce | flops 1536 | bytes 12288 | tf_op jit(solution)/shard_map/psum | solution.py:136
  267.7 6.8 %psum.51 = f32[768]{0:T(1024)S(1)} all-reduce(f32[768]{0:T(1024)S(1)} %get-tuple-element.51), channel_id=1, replica_groups=mesh['basin'=8,'event'=4] {'event'}, use_global_device_ids=true, to_apply=%region_20.0 | all-reduce | flops 768 | bytes 6144 | tf_op jit(solution)/shard_map/psum | solution.py:138
  274.5 20.5 %psum.52 = f32[768]{0:T(1024)} all-reduce(f32[768]{0:T(1024)S(1)} %psum.51), channel_id=1, replica_groups=mesh['basin'=8,'event'=4] {'basin'}, use_global_device_ids=true, to_apply=%region_21.0 | all-reduce | flops 768 | bytes 6144 | tf_op jit(solution)/shard_map/psum | solution.py:138
  295.0 132.2 %all-reduce.15.cloned.1.call-done = f32[768,768]{1,0:T(8,128)} async-done(((f32[768,768]{1,0:T(8,128)}), f32[768,768]{1,0:T(8,128)}) %all-reduce.15.cloned.1.call-update) | async-done | bytes 2359312 | tf_op jit(solution)/shard_map/psum | solution.py:136
  428.8 3.2 copy.97
  (153 shorter events, 71.4 us)
Async XLA Ops:
  7.2 2.7 copy-start
  7.2 2.5 copy-start.27
  7.2 2.5 copy-start.24
  7.2 2.6 copy-start.28
  9.7 2.2 copy-start.3
  9.8 5.0 %copy-start.18 = (f32[1536]{0:T(1024)}, f32[1536]{0:T(1024)S(1)}, u32[]{:S(2)}) copy-start(f32[1536]{0:T(1024)S(1)} %select_reduce_fusion) | copy-start | bytes 18436
  9.9 4.2 copy-start.19
  11.9 2.1 copy-start.1
  14.1 1.5 copy-start.2
  14.1 1.8 copy-start.25
  14.9 27.6 %copy-start.4 = (f32[3,32,1536]{2,1,0:T(8,128)S(1)}, f32[3,32,1536]{2,1,0:T(8,128)}, u32[]{:S(2)}) copy-start(f32[3,32,1536]{2,1,0:T(8,128)} %param.30) | copy-start | bytes 1769476
  18.8 19.3 %all-to-all-start = ((f32[8,1,768]{2,1,0:T(1,128)}), f32[8,1,768]{2,1,0:T(1,128)}, u32[]{:S(2)}, u32[]{:S(2)}) async-start(f32[8,1,768]{2,1,0:T(1,128)} %reshape.288), calls=%async_computation | async-start | bytes 49152 | tf_op jit(solution)/shard_map/all_to_all | solution.py:104
  42.5 1.8 copy-start.11
  42.5 23.0 %copy-start.22 = (s32[192,1]{0,1:T(1,128)S(1)}, s32[192,1]{0,1:T(1,128)}, u32[]{:S(2)}) copy-start(s32[192,1]{0,1:T(1,128)} %compare_select_fusion.2) | copy-start | bytes 2308
  48.2 16.5 %all-to-all-start.1 = ((f32[8,1,768]{2,1,0:T(1,128)}), f32[8,1,768]{2,1,0:T(1,128)S(1)}, u32[]{:S(2)}, u32[]{:S(2)}) async-start(f32[8,1,768]{2,1,0:T(1,128)} %reshape.290), calls=%async_computation.1 | async-start | bytes 49152 | tf_op jit(solution)/shard_map/all_to_all | solution.py:104
  67.9 28.3 %copy-start.6 = (f32[32,1536]{1,0:T(8,128)S(1)}, f32[32,1536]{1,0:T(8,128)}, u32[]{:S(2)}) copy-start(f32[32,1536]{1,0:T(8,128)} %param.31) | copy-start | bytes 589828
  67.9 28.3 %copy-start.13 = (f32[1536]{0:T(1024)S(1)}, f32[1536]{0:T(1024)}, u32[]{:S(2)}) copy-start(f32[1536]{0:T(1024)} %get-tuple-element.46) | copy-start | bytes 18436
  68.0 28.3 %copy-start.14 = (f32[1536]{0:T(1024)S(1)}, f32[1536]{0:T(1024)}, u32[]{:S(2)}) copy-start(f32[1536]{0:T(1024)} %get-tuple-element.50) | copy-start | bytes 18436
  73.3 17.8 %all-to-all-start.2 = ((f32[8,1,768]{2,1,0:T(1,128)}), f32[8,1,768]{2,1,0:T(1,128)S(1)}, u32[]{:S(2)}, u32[]{:S(2)}) async-start(f32[8,1,768]{2,1,0:T(1,128)} %reshape.292), calls=%async_computation.2 | async-start | bytes 49152 | tf_op jit(solution)/shard_map/all_to_all | solution.py:104
  97.3 26.1 %copy-start.5 = (f32[32,1536]{1,0:T(8,128)S(1)}, f32[32,1536]{1,0:T(8,128)}, u32[]{:S(2)}) copy-start(f32[32,1536]{1,0:T(8,128)} %get-tuple-element.45) | copy-start | bytes 589828
  103.3 13.4 %all-to-all-start.3 = ((f32[8,1,768]{2,1,0:T(1,128)}), f32[8,1,768]{2,1,0:T(1,128)}, u32[]{:S(2)}, u32[]{:S(2)}) async-start(f32[8,1,768]{2,1,0:T(1,128)} %reshape.294), calls=%async_computation.3 | async-start | bytes 49152 | tf_op jit(solution)/shard_map/all_to_all | solution.py:122
  132.7 12.7 %all-to-all-start.4 = ((f32[8,1,768]{2,1,0:T(1,128)}), f32[8,1,768]{2,1,0:T(1,128)}, u32[]{:S(2)}, u32[]{:S(2)}) async-start(f32[8,1,768]{2,1,0:T(1,128)} %reshape.296), calls=%async_computation.4 | async-start | bytes 49152 | tf_op jit(solution)/shard_map/all_to_all | solution.py:122
  156.3 16.9 %copy-start.17 = (f32[1536]{0:T(1024)S(1)}, f32[1536]{0:T(1024)}, u32[]{:S(2)}) copy-start(f32[1536]{0:T(1024)} %copy-done.16) | copy-start | bytes 18436
  158.0 12.2 %all-to-all-start.5 = ((f32[8,1,768]{2,1,0:T(1,128)}), f32[8,1,768]{2,1,0:T(1,128)S(1)}, u32[]{:S(2)}, u32[]{:S(2)}) async-start(f32[8,1,768]{2,1,0:T(1,128)} %reshape.298), calls=%async_computation.5 | async-start | bytes 49152 | tf_op jit(solution)/shard_map/all_to_all | solution.py:122
  163.5 49.5 %all-reduce.11.cloned.1.call-start = ((), (), s32[]{:S(2)}) async-start(), calls=%async_computation.6 | async-start | bytes 196608 | tf_op jit(solution)/shard_map/psum | solution.py:138
  174.1 6.9 %copy-start.15 = (bf16[1536,32]{0,1:T(8,128)(2,1)S(1)}, bf16[1536,32]{0,1:T(8,128)(2,1)}, u32[]{:S(2)}) copy-start(bf16[1536,32]{0,1:T(8,128)(2,1)} %param.16) | copy-start | bytes 294916
  174.1 38.9 %copy-start.23 = (f32[768]{0:T(1024)S(1)}, f32[768]{0:T(1024)}, u32[]{:S(2)}) copy-start(f32[768]{0:T(1024)} %convert_element_type.30) | copy-start | bytes 9220
  174.2 38.9 %copy-start.29 = (f32[768]{0:T(1024)S(1)}, f32[768]{0:T(1024)}, u32[]{:S(2)}) copy-start(f32[768]{0:T(1024)} %param.18) | copy-start | bytes 9220
  182.2 112.8 %all-reduce.13.cloned.1.call-start = ((), (), s32[]{:S(2)}) async-start(), calls=%async_computation.7 | async-start | bytes 196608 | tf_op jit(solution)/shard_map/psum | solution.py:138
  213.0 7.8 %copy-start.8 = (f32[32,1536]{1,0:T(8,128)S(1)}, f32[32,1536]{1,0:T(8,128)}, u32[]{:S(2)}) copy-start(f32[32,1536]{1,0:T(8,128)} %copy-done.7) | copy-start | bytes 589828
  213.0 7.8 %copy-start.10 = (f32[32,1536]{1,0:T(8,128)S(1)}, f32[32,1536]{1,0:T(8,128)}, u32[]{:S(2)}) copy-start(f32[32,1536]{1,0:T(8,128)} %copy-done.9) | copy-start | bytes 589828
  213.0 214.3 %all-reduce.15.cloned.1.call-start = ((), (), s32[]{:S(2)}) async-start(), calls=%async_computation.8 | async-start | bytes 4718592 | tf_op jit(solution)/shard_map/psum | solution.py:136
  (7 other events, 5.6 us)
Sparse Core Ops, SparseCore 0:
  182.3 30.5 all-reduce.10
  216.7 69.4 all-reduce.12
  293.2 133.9 all-reduce.14
